TPU v7x, 32 devices: a whole 2x2x4 slice. The times are simulated.
32 devices in a mesh: rows: 8 (over y, x, core), section: 4 (over z).
Axes of the slice: x: 2, y: 2, z: 4, core: 2. Of those that a mesh axis runs over, the one named last changes fastest.
Arguments:
- start_vec: float32 [16384, 2, 256], P('rows'), may hold values from -6 to 6
- left_vec: float32 [16384, 2, 256], P('rows'), may hold values from -6 to 6
- hamil: bfloat16 [128, 16, 2, 128, 128], P('rows', 'section'), may hold values from -0.109375 to 0.109375
- cols: int32 [128, 16], P('rows', 'section'), may hold values from 0 to 127, as said below
- live: int32 [128, 4], P('rows', 'section'), may hold values from 1 to 4, as said below
Outputs:
- moments: float32 [5, 256], replicated
- last_vec: float32 [16384, 2, 256], P('rows')
- before_vec: float32 [16384, 2, 256], P('rows')
Inputs may be any that keep to these rules, and one draw needn't show every extreme that they name: `cols`: each block column lies within 16 of its block row; slot 0 of every block row is the block row itself; a column may repeat in a row, and then its blocks add. `live`: loads differ between row groups.
All inputs are finite; a program needn't handle non-finite values.
Results may differ from a plain program's by a relative error of at most 0.0028.
Values may be sent and summed in bfloat16 or wider, within the bound.
A program may use at most 128 MiB of HBM per device.

v0:
```python
import jax
import jax.numpy as jnp
from jax import lax
from jax.sharding import PartitionSpec as P

REACH = 16
STEPS = 4


def padded(cells, sides, width):
    for axis, dim in sides:
        count = lax.axis_size(axis)
        ends = count - 1
        head = lax.slice_in_dim(cells, 0, width, axis=dim)
        tail = lax.slice_in_dim(cells, cells.shape[dim] - width, cells.shape[dim], axis=dim)
        cells = jnp.concatenate(
            [
                lax.ppermute(tail, axis, [(i, (i + 1) % count) for i in range(ends)]),
                cells,
                lax.ppermute(head, axis, [((i + 1) % count, i) for i in range(ends)]),
            ],
            axis=dim,
        )
    return cells


def complex_parts(out):
    real_part = out[:, 0, :, 0] - out[:, 1, :, 1]
    imag_part = out[:, 0, :, 1] + out[:, 1, :, 0]
    return jnp.stack([real_part, imag_part], axis=2)


def body(start_vec, left_vec, hamil, cols, live):
    row_blocks, slot_count = cols.shape
    block_size = hamil.shape[-1]
    base = lax.axis_index("rows") * row_blocks
    panel_index = cols - base + REACH
    mask_bf = (jnp.arange(slot_count)[None, :] < live).astype(jnp.bfloat16)
    scale = 1.0 / (2.0 * block_size * row_blocks) ** 0.5
    current = start_vec
    previous = start_vec
    table = [jnp.sum(left_vec * current, axis=(0, 1))]
    for step in range(STEPS):
        extended = padded(current.astype(jnp.bfloat16), (("rows", 0),), REACH * block_size)
        all_cols = extended.shape[2]
        blocks = extended.reshape(-1, block_size, 2, all_cols)
        panels = jnp.take(blocks, panel_index, axis=0) * mask_bf[:, :, None, None, None]
        out = jnp.einsum("bkqij,bkjpc->bqipc", hamil, panels, preferred_element_type=jnp.float32)
        summed = lax.psum(
            complex_parts(out).reshape(row_blocks * block_size, 2, all_cols), "section"
        )
        fresh = summed if step == 0 else 2.0 * summed - previous
        previous, current = (current, fresh)
        table.append(jnp.sum(left_vec * current, axis=(0, 1)))
    partial_value = jnp.stack(table, axis=0)
    moments = lax.psum(partial_value, "rows") * scale
    return (moments, current, previous)


def solution(mesh):
    return jax.shard_map(
        body,
        mesh=mesh,
        in_specs=(
            P("rows", None, None),
            P("rows", None, None),
            P("rows", "section", None, None, None),
            P("rows", "section"),
            P("rows", "section"),
        ),
        out_specs=(P(), P("rows", None, None), P("rows", None, None)),
        check_vma=False,
    )
```

profile of v0, /device:TPU:0, one launch (start us, length us, event | category | flops | bytes accessed | tf_op | source)
XLA Modules:
  0.0 1040.9 jit_solution(10793872942615279801)
XLA Ops:
  15.9 4.4 collective-permute-done.1
  26.8 8.3 gather_fusion
  35.1 10.4 %fusion.12 = f32[16,2,128,2,256]{4,2,1,3,0:T(8,128)} fusion(bf16[16,4,128,2,256]{4,2,3,1,0:T(8,128)(2,1)} %bitcast.79, pred[16,4]{1,0:T(8,128)(4,1)S(1)} %copy.76, bf16[16,4]{1,0:T(8,128)(2,1)S(1)} %fusion.28, bf16[16,4,2,128,128]{4,3,2,1,0:T(8,128)(2,1)} %param.9), kind=kOutput, calls=%fused_computation.37 | convolution fusion | flops 2155872256 | bytes 20971712 | tf_op jit(solution)/shard_map/bkqij,bkjpc->bqipc/dot_general | solution.py:48
  45.5 4.1 slice_subtract_fusion.3
  52.0 196.6 %all-reduce.5.cloned.1.call-done = f32[2048,2,256]{2,0,1:T(8,128)} async-done(((f32[2048,2,256]{2,0,1:T(8,128)}), f32[2048,2,256]{2,0,1:T(8,128)}) %all-reduce.5.cloned.1.call-update) | async-done | bytes 4194320 | tf_op jit(solution)/shard_map/psum | solution.py:49
  260.0 13.9 %pad_maximum_fusion.1 = bf16[6144,2,256]{2,0,1:T(8,128)(2,1)S(1)} fusion(bf16[2048,2,256]{2,0,1:T(8,128)(2,1)S(1)} %collective-permute-done.3, bf16[2048,2,256]{2,0,1:T(8,128)(2,1)S(1)} %convert_element_type.21, bf16[2048,2,256]{2,0,1:T(8,128)(2,1)S(1)} %collective-permute-done.2), kind=kLoop, calls=%fused_computation.21 | loop fusion | flops 18874368 | bytes 12582912 | tf_op jit(solution)/shard_map/concatenate | solution.py:16
  277.1 8.3 gather_fusion.1
  285.4 10.4 %fusion.15 = f32[16,2,128,2,256]{4,2,1,3,0:T(8,128)} fusion(bf16[16,4,128,2,256]{4,2,3,1,0:T(8,128)(2,1)} %bitcast.80, pred[16,4]{1,0:T(8,128)(4,1)S(1)} %copy.76, bf16[16,4]{1,0:T(8,128)(2,1)S(1)} %fusion.28, bf16[16,4,2,128,128]{4,3,2,1,0:T(8,128)(2,1)} %param.9), kind=kOutput, calls=%fused_computation.38 | convolution fusion | flops 2155872256 | bytes 20971712 | tf_op jit(solution)/shard_map/bkqij,bkjpc->bqipc/dot_general | solution.py:48
  295.8 4.1 slice_subtract_fusion.2
  302.2 194.3 %all-reduce.7.cloned.1.call-done = f32[2048,2,256]{2,0,1:T(8,128)} async-done(((f32[2048,2,256]{2,0,1:T(8,128)}), f32[2048,2,256]{2,0,1:T(8,128)}) %all-reduce.7.cloned.1.call-update) | async-done | bytes 4194320 | tf_op jit(solution)/shard_map/psum | solution.py:49
  509.7 14.0 %pad_maximum_fusion.2 = bf16[6144,2,256]{2,0,1:T(8,128)(2,1)S(1)} fusion(bf16[2048,2,256]{2,0,1:T(8,128)(2,1)S(1)} %collective-permute-done.5, bf16[2048,2,256]{2,0,1:T(8,128)(2,1)S(1)} %fusion.29, bf16[2048,2,256]{2,0,1:T(8,128)(2,1)S(1)} %collective-permute-done.4), kind=kLoop, calls=%fused_computation.22 | loop fusion | flops 18874368 | bytes 12582912 | tf_op jit(solution)/shard_map/concatenate | solution.py:16
  526.8 8.3 gather_fusion.2
  535.1 10.4 %fusion.18 = f32[16,2,128,2,256]{4,2,1,3,0:T(8,128)} fusion(bf16[16,4,128,2,256]{4,2,3,1,0:T(8,128)(2,1)} %bitcast.81, pred[16,4]{1,0:T(8,128)(4,1)S(1)} %copy.76, bf16[16,4]{1,0:T(8,128)(2,1)S(1)} %fusion.28, bf16[16,4,2,128,128]{4,3,2,1,0:T(8,128)(2,1)} %param.9), kind=kOutput, calls=%fused_computation.39 | convolution fusion | flops 2155872256 | bytes 20971712 | tf_op jit(solution)/shard_map/bkqij,bkjpc->bqipc/dot_general | solution.py:48
  552.0 194.3 %all-reduce.9.cloned.1.call-done = f32[2048,2,256]{2,0,1:T(8,128)} async-done(((f32[2048,2,256]{2,0,1:T(8,128)}), f32[2048,2,256]{2,0,1:T(8,128)}) %all-reduce.9.cloned.1.call-update) | async-done | bytes 4194320 | tf_op jit(solution)/shard_map/psum | solution.py:49
  746.3 6.1 fusion.30
  761.4 13.8 %pad_maximum_fusion.3 = bf16[6144,2,256]{2,0,1:T(8,128)(2,1)S(1)} fusion(bf16[2048,2,256]{2,0,1:T(8,128)(2,1)S(1)} %collective-permute-done.7, bf16[2048,2,256]{2,0,1:T(8,128)(2,1)S(1)} %get-tuple-element.12, bf16[2048,2,256]{2,0,1:T(8,128)(2,1)S(1)} %collective-permute-done.6), kind=kLoop, calls=%fused_computation.23 | loop fusion | flops 18874368 | bytes 12582912 | tf_op jit(solution)/shard_map/concatenate | solution.py:16
  778.4 8.3 gather_fusion.3
  786.7 10.4 %fusion.21 = f32[16,2,128,2,256]{4,2,1,3,0:T(8,128)} fusion(bf16[16,4,128,2,256]{4,2,3,1,0:T(8,128)(2,1)} %bitcast.78, pred[16,4]{1,0:T(8,128)(4,1)S(1)} %copy.76, bf16[16,4]{1,0:T(8,128)(2,1)S(1)} %fusion.28, bf16[16,4,2,128,128]{4,3,2,1,0:T(8,128)(2,1)} %param.9), kind=kOutput, calls=%fused_computation.40 | convolution fusion | flops 2155872256 | bytes 20971712 | tf_op jit(solution)/shard_map/bkqij,bkjpc->bqipc/dot_general | solution.py:48
  803.5 6.6 multiply_reduce_fusion.4
  810.1 12.5 %copy.103 = f32[2048,2,256]{2,1,0:T(2,128)} copy(f32[2048,2,256]{2,0,1:T(8,128)S(1)} %copy-done) | data formatting | bytes 8388608
  822.6 175.3 %all-reduce.11.cloned.1.call-done = f32[2048,2,256]{2,0,1:T(8,128)} async-done(((f32[2048,2,256]{2,0,1:T(8,128)}), f32[2048,2,256]{2,0,1:T(8,128)}) %all-reduce.11.cloned.1.call-update) | async-done | bytes 4194320 | tf_op jit(solution)/shard_map/psum | solution.py:49
  997.8 9.4 multiply_reduce_fusion
  1007.2 12.2 %copy.102 = f32[2048,2,256]{2,1,0:T(2,128)} copy(f32[2048,2,256]{2,0,1:T(8,128)S(1)} %get-tuple-element.11) | data formatting | bytes 8388608
  1019.4 13.9 %psum.39 = f32[5,256]{1,0:T(8,128)S(1)} all-reduce(f32[5,256]{1,0:T(8,128)S(1)} %stack.47), channel_id=1, replica_groups=mesh['rows'=8,'section'=4] {'rows'}, use_global_device_ids=true, to_apply=%region_9.11 | all-reduce | flops 1280 | bytes 10240 | tf_op jit(solution)/shard_map/psum | solution.py:56
  (51 shorter events, 76.3 us)
Async XLA Ops:
  7.2 7.5 copy-start.1
  7.2 7.7 copy-start.2
  7.2 241.4 %all-reduce.5.cloned.1.call-start = ((), (), s32[]{:S(2)}) async-start(), calls=%async_computation | async-start | bytes 8388608 | tf_op jit(solution)/shard_map/psum | solution.py:49
  9.6 6.3 collective-permute-start
  13.3 7.0 collective-permute-start.1
  51.9 444.6 %all-reduce.7.cloned.1.call-start = ((), (), s32[]{:S(2)}) async-start(), calls=%async_computation.1 | async-start | bytes 8388608 | tf_op jit(solution)/shard_map/psum | solution.py:49
  250.9 5.5 collective-permute-start.2
  252.8 7.2 collective-permute-start.3
  302.2 444.1 %all-reduce.9.cloned.1.call-start = ((), (), s32[]{:S(2)}) async-start(), calls=%async_computation.2 | async-start | bytes 8388608 | tf_op jit(solution)/shard_map/psum | solution.py:49
  500.6 5.5 collective-permute-start.4
  502.5 7.2 collective-permute-start.5
  551.9 445.9 %all-reduce.11.cloned.1.call-start = ((), (), s32[]{:S(2)}) async-start(), calls=%async_computation.3 | async-start | bytes 8388608 | tf_op jit(solution)/shard_map/psum | solution.py:49
  752.4 5.5 collective-permute-start.6
  754.2 7.2 collective-permute-start.7
  803.5 6.6 copy-start
Sparse Core Ops, SparseCore 0:
  52.1 196.4 all-reduce.4
  302.3 194.1 all-reduce.6
  552.1 194.1 all-reduce.8
  803.6 194.1 all-reduce.10
where the time goes:
time: 1050 us; the launch traced here: 1040 us
  waiting for transfers between devices  783 us (75%)
  other arithmetic  99.7 us (9%)
  local copies, waits for them, and re-layouts  73.1 us (7%)
  matrix products  41.7 us (4%)
  starting transfers between devices  15.4 us (1%)
  between operations  14.4 us (1%)
  blocking collectives  13.9 us (1%)
    psum x4, waiting for transfers between devices, body(): lax.psum(complex_parts(out).reshape(row_blocks * block_size, 2, all_cols)...  760 us
    concatenate x4, other arithmetic, padded(): jnp.concatenate([lax.ppermute(tail, axis, [(i, (i + 1) % count) for i in...  45 us
    dot_general x4, matrix products, body(): jnp.einsum('bkqij,bkjpc->bqipc', hamil, panels, preferred_element_type=jn...  41.7 us
    gather x4, local copies, waits for them, and re-layouts, body(): jnp.take(blocks, panel_index, axis=0) * mask_bf[:, :, None, None, None]  33.2 us
    unnamed x9, local copies, waits for them, and re-layouts  27.1 us
  transfers between devices with their start and end apart: 12, of which 12 were waited for; matrix products, arithmetic and copies ran while one was open for 2% of the time, Pallas kernels for 0%

commit v1 on v0

v1 whole, which is shorter than its diff:
```python
import functools

import jax
import jax.numpy as jnp
from jax import lax
from jax.experimental import pallas as pl
from jax.experimental.pallas import tpu as pltpu
from jax.sharding import PartitionSpec as P

MESH = pl.DeviceIdType.MESH
STEPS = 4
GROUP = 16


def kernel(
    nr, ns, slots, scale,
    idx, v0, own0, left, hm,
    mom_out, t3_out, t4_out,
    ext0, ext1, ext2, ext3, last, hrecv, hc, tbuf, mloc, msec, mrow,
    up_sem, down_sem, right_sem, left_sem, own_recv, lhalo_recv, rhalo_recv,
    h_send, h_recv, m_send, m_recv, n_send, n_recv, local_sem,
):
    g = lax.axis_index("rows")
    s = lax.axis_index("section")
    rb = v0.shape[0]
    R = rb // ns
    bs = hm.shape[-1]
    sc = hm.shape[1]
    bufs = (ext0, ext1, ext2, ext3, last)

    barrier = pltpu.get_barrier_semaphore()

    @pl.loop(1, ns)
    def _(d):
        pl.semaphore_signal(barrier, inc=1, device_id=(g, lax.rem(s + d, ns)), device_id_type=MESH)

    @pl.loop(1, nr)
    def _(d):
        pl.semaphore_signal(barrier, inc=1, device_id=(lax.rem(g + d, nr), s), device_id_type=MESH)

    pl.semaphore_wait(barrier, ns + nr - 2)

    def own(n, c):
        return bufs[n].at[c] if n == STEPS else bufs[n].at[rb + c]

    def remote(src, dst, ss, rs, dev):
        return pltpu.make_async_remote_copy(
            src_ref=src, dst_ref=dst, send_sem=ss, recv_sem=rs, device_id=dev, device_id_type=MESH
        )

    def up(n, c):
        return remote(own(n, c), own(n, c), up_sem.at[n - 1, c], own_recv.at[n - 1, c], (g, s + 1))

    def down(n, c):
        return remote(own(n, c), own(n, c), down_sem.at[n - 1, c], own_recv.at[n - 1, c], (g, s - 1))

    def right(n, c):
        src = v0.at[c] if n == 0 else own(n, c)
        return remote(src, bufs[n].at[c], right_sem.at[n, c], lhalo_recv.at[n, c], (g + 1, s))

    def leftward(n, c):
        src = v0.at[c] if n == 0 else own(n, c)
        return remote(src, bufs[n].at[2 * rb + c], left_sem.at[n, c], rhalo_recv.at[n, c], (g - 1, s))

    def each(n, c, act):
        k = c // R
        if n > 0:
            @pl.when((k <= s) & (s < ns - 1))
            def _():
                act(up(n, c))

            @pl.when((k >= s) & (s > 0))
            def _():
                act(down(n, c))
        if n < STEPS:
            @pl.when((k >= s) & (g < nr - 1))
            def _():
                act(right(n, c))

            @pl.when((k <= s) & (g > 0))
            def _():
                act(leftward(n, c))

    def halos(n):
        @pl.loop(0, rb)
        def _(c):
            k = c // R

            @pl.when((k >= s) & (g > 0))
            def _():
                right(n, c).wait_recv()

            @pl.when((k <= s) & (g < nr - 1))
            def _():
                leftward(n, c).wait_recv()

    def coupling(d, r):
        to = lax.rem(s + d, ns)
        return remote(hm.at[to * R + r], hrecv.at[s, r], h_send.at[to, r], h_recv.at[s, r], (g, to))

    def arrived(d, r):
        at = lax.rem(s + d, ns)
        return remote(hm.at[r], hrecv.at[at, r], h_send.at[at, r], h_recv.at[at, r], (g, at))

    @pl.loop(0, R)
    def _(r):
        @pl.loop(1, ns)
        def _(d):
            coupling(d, r).start()

    @pl.loop(0, rb)
    def _(c):
        each(0, c, lambda x: x.start())

    copy_h = pltpu.make_async_copy(hm.at[pl.ds(s * R, R)], hrecv.at[s], local_sem.at[0])
    copy_v = pltpu.make_async_copy(v0, ext0.at[pl.ds(rb, rb)], local_sem.at[1])
    copy_h.start()
    copy_v.start()
    mloc[...] = jnp.zeros_like(mloc)

    def moment(n, r, t):
        mloc[n : n + 1, :] += jnp.sum(left[r] * t, axis=0, keepdims=True)

    @pl.loop(0, R)
    def _(r):
        moment(0, r, own0[r])
        tbuf[0, r] = own0[r]

    copy_h.wait()
    copy_v.wait()
    halos(0)

    def build(r):
        @pl.loop(0, slots)
        def _(j):
            src, k = j // sc, j % sc
            hr = hrecv[src, r, k, 0]
            hi = hrecv[src, r, k, 1]
            first = pl.ds(pl.multiple_of(j * 2 * bs, bs), bs)
            second = pl.ds(pl.multiple_of(j * 2 * bs + bs, bs), bs)
            hc[r, 0:bs, first] = hr
            hc[r, 0:bs, second] = -hi
            hc[r, bs : 2 * bs, first] = hi
            hc[r, bs : 2 * bs, second] = hr

    group = min(GROUP, slots)

    def product(n, r):
        def part(p):
            base = p * group
            rhs = jnp.concatenate(
                [bufs[n - 1][idx[r * slots + base + u]] for u in range(group)], axis=0
            )
            lhs = hc[r, :, pl.ds(pl.multiple_of(base * 2 * bs, 2 * bs), group * 2 * bs)]
            return jnp.dot(lhs, rhs, preferred_element_type=jnp.float32)

        if slots == group:
            return part(0)
        zero = jnp.zeros((2 * bs, v0.shape[-1]), jnp.float32)
        return lax.fori_loop(0, slots // group, lambda p, a: a + part(p), zero)

    for n in range(1, STEPS + 1):
        @pl.loop(0, R)
        def _(r, n=n):
            if n == 1:
                @pl.loop(1, ns)
                def _(d):
                    arrived(d, r).wait_recv()

                build(r)
            t = product(n, r)
            if n > 1:
                t = 2.0 * t - tbuf[n % 2, r]
            tbuf[n % 2, r] = t
            c = s * R + r
            if n == STEPS:
                bufs[n][c] = t.astype(jnp.bfloat16)
            else:
                bufs[n][rb + c] = t.astype(jnp.bfloat16)
            each(n, c, lambda x: x.start())
            moment(n, r, t)

        if n == STEPS:
            msec[s] = mloc[...]

            @pl.loop(1, ns)
            def _(d):
                to = lax.rem(s + d, ns)
                remote(mloc, msec.at[s], m_send.at[to], m_recv.at[s], (g, to)).start()

        @pl.loop(1, ns)
        def _(d, n=n):
            @pl.loop(0, R)
            def _(r):
                @pl.when(s - d >= 0)
                def _():
                    c = (s - d) * R + r
                    up(n, c).wait_recv()
                    each(n, c, lambda x: x.start())

                @pl.when(s + d < ns)
                def _():
                    c = (s + d) * R + r
                    down(n, c).wait_recv()
                    each(n, c, lambda x: x.start())

        if n < STEPS:
            halos(n)
        if n == STEPS - 1:
            pltpu.make_async_copy(ext3.at[pl.ds(rb, rb)], t3_out, local_sem.at[2]).start()

    copy_t = pltpu.make_async_copy(last, t4_out, local_sem.at[3])
    copy_t.start()

    @pl.loop(1, ns)
    def _(d):
        at = lax.rem(s + d, ns)
        remote(mloc, msec.at[at], m_send.at[at], m_recv.at[at], (g, at)).wait()

    total = msec[0]
    for i in range(1, ns):
        total += msec[i]
    mrow[g] = total

    @pl.loop(1, nr)
    def _(d):
        to = lax.rem(g + d, nr)
        remote(mrow.at[g], mrow.at[g], n_send.at[to], n_recv.at[g], (to, s)).start()

    @pl.loop(1, nr)
    def _(d):
        at = lax.rem(g + d, nr)
        remote(mrow.at[at], mrow.at[at], n_send.at[at], n_recv.at[at], (at, s)).wait()

    total = mrow[0]
    for i in range(1, nr):
        total += mrow[i]
    mom_out[...] = total * scale

    @pl.loop(0, R)
    def _(r):
        @pl.loop(1, ns)
        def _(d):
            coupling(d, r).wait_send()

    for n in range(STEPS + 1):
        @pl.loop(0, rb)
        def _(c, n=n):
            each(n, c, lambda x: x.wait_send())

    pltpu.make_async_copy(ext3.at[pl.ds(rb, rb)], t3_out, local_sem.at[2]).wait()
    copy_t.wait()


def body(nr, ns, start_vec, left_vec, hamil, cols, live):
    rb, sc = cols.shape
    bs = hamil.shape[-1]
    width = start_vec.shape[-1]
    R = rb // ns
    slots = sc * ns
    s = lax.axis_index("section")
    base = lax.axis_index("rows") * rb
    scale = 1.0 / (2.0 * bs * rb) ** 0.5

    def panels(x):
        count = x.shape[0] // bs
        return x.reshape(count, bs, 2, width).transpose(0, 2, 1, 3).reshape(count, 2 * bs, width)

    def owned(x):
        return panels(lax.dynamic_slice_in_dim(x, s * (R * bs), R * bs, axis=0))

    v0 = panels(start_vec.astype(jnp.bfloat16))
    mask = jnp.arange(sc)[None, :] < live
    hm = jnp.where(mask[:, :, None, None, None], hamil, jnp.zeros((), hamil.dtype))
    every = lax.all_gather(cols, "section", axis=1, tiled=True)
    idx = (lax.dynamic_slice_in_dim(every, s * R, R, axis=0) - base + rb).reshape(-1)

    dma = pltpu.SemaphoreType.DMA
    vmem = pl.BlockSpec(memory_space=pltpu.VMEM)
    anywhere = pl.BlockSpec(memory_space=pl.ANY)
    bf, f32 = jnp.bfloat16, jnp.float32
    ext = pltpu.VMEM((3 * rb, 2 * bs, width), bf)
    mom, t3, t4 = pl.pallas_call(
        functools.partial(kernel, nr, ns, slots, scale),
        out_shape=(
            jax.ShapeDtypeStruct((8, width), f32),
            jax.ShapeDtypeStruct((rb, 2 * bs, width), bf),
            jax.ShapeDtypeStruct((rb, 2 * bs, width), bf),
        ),
        in_specs=[pl.BlockSpec(memory_space=pltpu.SMEM), anywhere, vmem, vmem, anywhere],
        out_specs=(vmem, anywhere, anywhere),
        scratch_shapes=[
            ext, ext, ext, ext,
            pltpu.VMEM((rb, 2 * bs, width), bf),
            pltpu.VMEM((ns, R, sc, 2, bs, bs), bf),
            pltpu.VMEM((R, 2 * bs, slots * 2 * bs), bf),
            pltpu.VMEM((2, R, 2 * bs, width), f32),
            pltpu.VMEM((8, width), f32),
            pltpu.VMEM((ns, 8, width), f32),
            pltpu.VMEM((nr, 8, width), f32),
            dma((STEPS, rb)), dma((STEPS, rb)), dma((STEPS, rb)), dma((STEPS, rb)),
            dma((STEPS, rb)), dma((STEPS, rb)), dma((STEPS, rb)),
            dma((ns, R)), dma((ns, R)),
            dma((ns,)), dma((ns,)), dma((nr,)), dma((nr,)), dma((4,)),
        ],
        compiler_params=pltpu.CompilerParams(
            collective_id=0, has_side_effects=True, vmem_limit_bytes=56 * 2**20
        ),
    )(idx, v0, owned(start_vec), owned(left_vec), hm)

    def whole(x):
        return (
            x.astype(f32).reshape(rb, 2, bs, width).transpose(0, 2, 1, 3).reshape(rb * bs, 2, width)
        )

    return mom[: STEPS + 1], whole(t4), whole(t3)


def solution(mesh):
    nr, ns = mesh.shape["rows"], mesh.shape["section"]
    return jax.shard_map(
        functools.partial(body, nr, ns),
        mesh=mesh,
        in_specs=(
            P("rows", None, None),
            P("rows", None, None),
            P("rows", "section", None, None, None),
            P("rows", "section"),
            P("rows", "section"),
        ),
        out_specs=(P(), P("rows", None, None), P("rows", None, None)),
        check_vma=False,
    )
```

time: 1050 us -> 275 us (0.26)
  waiting for transfers between devices: 783 us -> 0 us
  Pallas kernels: 0 us -> 234 us
  other arithmetic: 99.7 us -> 7.26 us
  local copies, waits for them, and re-layouts: 73.1 us -> 18.7 us
  matrix products: 41.7 us -> 0 us
  starting transfers between devices: 15.4 us -> 0 us
  between operations: 14.4 us -> 0.72 us
    psum x4 -> x0, waiting for transfers between devices: 760 us -> none  [body(): lax.psum(complex_parts(out).reshape(row_blocks * block_size, 2, all_cols)...]
    pallas_call x0 -> x1, Pallas kernels: none -> 234 us  [body(): pl.pallas_call(functools.partial(kernel, nr, ns, slots, scale), out_shape...]
    concatenate x4 -> x0, other arithmetic: 45 us -> none  [padded(): jnp.concatenate([lax.ppermute(tail, axis, [(i, (i + 1) % count) for i in...]
    dot_general x4 -> x0, matrix products: 41.7 us -> none  [body(): jnp.einsum('bkqij,bkjpc->bqipc', hamil, panels, preferred_element_type=jn...]
    gather x4 -> x0, local copies, waits for them, and re-layouts: 33.2 us -> none  [body(): jnp.take(blocks, panel_index, axis=0) * mask_bf[:, :, None, None, None]]
    unnamed x9 -> x12, local copies, waits for them, and re-layouts: 27.1 us -> 1.5 us
    ppermute x8 -> x0, waiting for transfers between devices: 22.2 us -> none  [the longest x4 15.1 us: padded(): lax.ppermute(head, axis, [((i + 1) % count, i) for i in range(ends)])]
    sub x4 -> x0, other arithmetic: 16.4 us -> none  [complex_parts(): real_part = out[:, 0, :, 0] - out[:, 1, :, 1]]
  transfers between devices with their start and end apart: 12 -> 0, of which waited for: 12 -> 0; matrix products, arithmetic and copies ran while one was open for 2% -> 0% of each run, Pallas kernels for 0% -> 0%
where the time goes in v1:
time: 275 us
  Pallas kernels  234 us (85%)
  local copies, waits for them, and re-layouts  18.7 us (7%)
  blocking collectives  13.7 us (5%)
  other arithmetic  7.26 us (3%)
    pallas_call x1, Pallas kernels, body(): pl.pallas_call(functools.partial(kernel, nr, ns, slots, scale), out_shape...  234 us
    all_gather x1, blocking collectives, body(): every = lax.all_gather(cols, 'section', axis=1, tiled=True)  13.7 us
    reshape x2, local copies, waits for them, and re-layouts, whole(): x.astype(f32).reshape(rb, 2, bs, width).transpose(0, 2, 1, 3)  10.5 us

profile of v1, /device:TPU:0, one launch (start us, length us, event | category | flops | bytes accessed | tf_op | source)
XLA Modules:
  0.0 274.7 jit_solution(1408562729839258932)
XLA Ops:
  0.6 0.7 iota_compare_fusion
  1.4 13.7 %all-gather = s32[4,4,16]{2,1,0:T(4,128)S(1)} all-gather(s32[1,4,16]{2,1,0:T(4,128)} %bitcast.42), channel_id=1, replica_groups=mesh['rows'=8,'section'=4] {'section'}, dimensions={0}, use_global_device_ids=true | all-gather | bytes 1280 | tf_op jit(solution)/shard_map/all_gather | solution.py:275
  15.0 0.1 subtract_add_fusion
  15.1 0.1 copy.31
  15.2 0.6 reshape.69.idx
  15.8 2.3 constant_dynamic-slice_fusion
  18.1 0.0 copy-start
  18.1 0.1 copy.30
  18.2 1.1 copy.25
  19.2 0.1 copy.29
  19.3 1.0 copy.23
  20.4 0.7 copy-done
  21.0 1.5 convert_element_type.2
  22.5 1.7 copy.21
  24.2 0.0 copy-done.1
  24.2 2.4 broadcast_select_fusion.hm
  26.6 234.4 %shard_map.79 = (f32[8,256]{1,0:T(8,128)}, bf16[16,256,256]{2,1,0:T(8,128)(2,1)}, bf16[16,256,256]{2,1,0:T(8,128)(2,1)}) custom-call(s32[64]{0:T(128)} %reshape.69.idx, bf16[16,256,256]{2,1,0:T(8,128)(2,1)} %bitcast.30, f32[4,256,256]{2,1,0:T(8,128)} %bitcast.32, f32[4,256,256]{2,1,0:T(8,128)} %bitcast.31, bf16[16,4,2,128,128]{4,3,2,1,0:T(8,128)(2,1)} %broadcast_select_fusion.hm), custom_call_target="tpu_custom_call" | custom-call | tf_op jit(solution)/shard_map/pallas_call | solution.py:283
  260.9 2.1 convert_bitcast_fusion.1
  263.1 5.3 %copy.26 = f32[16,128,2,256]{3,2,1,0:T(2,128)} copy(f32[16,128,2,256]{3,1,2,0:T(8,128)S(1)} %convert_bitcast_fusion.1) | data formatting | bytes 8388608 | tf_op jit(solution)/shard_map/reshape | solution.py:313
  268.3 0.5 convert_bitcast_fusion
  268.8 0.0 copy-start.3
  268.9 5.3 %copy.27 = f32[16,128,2,256]{3,2,1,0:T(2,128)} copy(f32[16,128,2,256]{3,1,2,0:T(8,128)S(1)} %convert_bitcast_fusion) | data formatting | bytes 8388608 | tf_op jit(solution)/shard_map/reshape | solution.py:313
  274.1 0.0 copy-done.3
  274.1 0.6 copy.33
  (3 shorter events, 0.0 us)
Async XLA Ops:
  18.1 2.9 %copy-start = (f32[2048,2,256]{2,1,0:T(2,128)S(1)}, f32[2048,2,256]{2,1,0:T(2,128)}, u32[]{:S(2)}) copy-start(f32[2048,2,256]{2,1,0:T(2,128)} %param.5) | copy-start | bytes 12582916
  21.0 3.2 %copy-start.1 = (bf16[16,4,2,128,128]{4,3,2,1,0:T(8,128)(2,1)S(1)}, bf16[16,4,2,128,128]{4,3,2,1,0:T(8,128)(2,1)}, u32[]{:S(2)}) copy-start(bf16[16,4,2,128,128]{4,3,2,1,0:T(8,128)(2,1)} %param.7) | copy-start | bytes 12582916
  263.1 5.3 %copy-start.2 = (bf16[16,256,256]{2,1,0:T(8,128)(2,1)S(1)}, bf16[16,256,256]{2,1,0:T(8,128)(2,1)}, u32[]{:S(2)}) copy-start(bf16[16,256,256]{2,1,0:T(8,128)(2,1)} %get-tuple-element.8) | copy-start | bytes 6291460
  268.8 5.3 %copy-start.3 = (f32[8,256]{1,0:T(8,128)S(1)}, f32[8,256]{1,0:T(8,128)}, u32[]{:S(2)}) copy-start(f32[8,256]{1,0:T(8,128)} %get-tuple-element.6) | copy-start | bytes 24580

commit v2 on v1

--- a/solution.py
+++ b/solution.py
@@ -14,15 +14,16 @@
 
 def kernel(
     nr, ns, slots, scale,
-    idx, v0, own0, left, hm,
+    code, start_hbm, left_hbm, hm,
     mom_out, t3_out, t4_out,
-    ext0, ext1, ext2, ext3, last, hrecv, hc, tbuf, mloc, msec, mrow,
+    stage, left_stage, codes, idx, ext0, ext1, ext2, ext3, last, hrecv, hc, tbuf, left, mloc, msec, mrow,
     up_sem, down_sem, right_sem, left_sem, own_recv, lhalo_recv, rhalo_recv,
-    h_send, h_recv, m_send, m_recv, n_send, n_recv, local_sem,
+    h_send, h_recv, c_send, c_recv, m_send, m_recv, n_send, n_recv, local_sem,
 ):
     g = lax.axis_index("rows")
     s = lax.axis_index("section")
-    rb = v0.shape[0]
+    rb = hm.shape[0]
+    width = start_hbm.shape[-1]
     R = rb // ns
     bs = hm.shape[-1]
     sc = hm.shape[1]
@@ -55,12 +56,10 @@
         return remote(own(n, c), own(n, c), down_sem.at[n - 1, c], own_recv.at[n - 1, c], (g, s - 1))
 
     def right(n, c):
-        src = v0.at[c] if n == 0 else own(n, c)
-        return remote(src, bufs[n].at[c], right_sem.at[n, c], lhalo_recv.at[n, c], (g + 1, s))
+        return remote(own(n, c), bufs[n].at[c], right_sem.at[n, c], lhalo_recv.at[n, c], (g + 1, s))
 
     def leftward(n, c):
-        src = v0.at[c] if n == 0 else own(n, c)
-        return remote(src, bufs[n].at[2 * rb + c], left_sem.at[n, c], rhalo_recv.at[n, c], (g - 1, s))
+        return remote(own(n, c), bufs[n].at[2 * rb + c], left_sem.at[n, c], rhalo_recv.at[n, c], (g - 1, s))
 
     def each(n, c, act):
         k = c // R
@@ -102,40 +101,69 @@
         at = lax.rem(s + d, ns)
         return remote(hm.at[r], hrecv.at[at, r], h_send.at[at, r], h_recv.at[at, r], (g, at))
 
+    @pl.loop(1, ns)
+    def _(d):
+        to = lax.rem(s + d, ns)
+        remote(code.at[to], codes.at[s], c_send.at[to], c_recv.at[s], (g, to)).start()
+
+    ahead = min(2, R)
+    for r in range(ahead):
+        @pl.loop(1, ns)
+        def _(d, r=r):
+            coupling(d, r).start()
+
+    copy_v = pltpu.make_async_copy(start_hbm, stage, local_sem.at[1])
+    copy_v.start()
+    copy_l = pltpu.make_async_copy(
+        left_hbm.at[pl.ds(s * (R * bs), R * bs)], left_stage, local_sem.at[4]
+    )
+    copy_l.start()
+    copy_h = pltpu.make_async_copy(hm.at[pl.ds(s * R, R)], hrecv.at[s], local_sem.at[0])
+    copy_h.start()
+    mloc[...] = jnp.zeros_like(mloc)
+    codes[s] = code[s]
+    copy_v.wait()
+
+    @pl.loop(0, rb)
+    def _(c):
+        for q in range(2):
+            part = stage[pl.ds(c * bs, bs), q, :]
+            ext0[rb + c, q * bs : (q + 1) * bs, :] = part.astype(jnp.bfloat16)
+        each(0, c, lambda x: x.start())
+
+    copy_l.wait()
+
+    def moment(n, r, t):
+        for q in range(2):
+            probe = left[r, q * bs : (q + 1) * bs, :]
+            mloc[n : n + 1, :] += jnp.sum(probe * t[q * bs : (q + 1) * bs], axis=0, keepdims=True)
+
     @pl.loop(0, R)
     def _(r):
-        @pl.loop(1, ns)
-        def _(d):
-            coupling(d, r).start()
-
-    @pl.loop(0, rb)
-    def _(c):
-        each(0, c, lambda x: x.start())
-
-    copy_h = pltpu.make_async_copy(hm.at[pl.ds(s * R, R)], hrecv.at[s], local_sem.at[0])
-    copy_v = pltpu.make_async_copy(v0, ext0.at[pl.ds(rb, rb)], local_sem.at[1])
-    copy_h.start()
-    copy_v.start()
-    mloc[...] = jnp.zeros_like(mloc)
-
-    def moment(n, r, t):
-        mloc[n : n + 1, :] += jnp.sum(left[r] * t, axis=0, keepdims=True)
-
-    @pl.loop(0, R)
-    def _(r):
-        moment(0, r, own0[r])
-        tbuf[0, r] = own0[r]
-
+        for q in range(2):
+            rows = slice(q * bs, (q + 1) * bs)
+            tbuf[0, r, rows, :] = stage[pl.ds((s * R + r) * bs, bs), q, :]
+            left[r, rows, :] = left_stage[pl.ds(r * bs, bs), q, :]
+        moment(0, r, tbuf[0, r])
+
+    @pl.loop(1, ns)
+    def _(d):
+        at = lax.rem(s + d, ns)
+        remote(code.at[at], codes.at[at], c_send.at[at], c_recv.at[at], (g, at)).wait()
+
+    copy_c = pltpu.make_async_copy(codes, idx, local_sem.at[5])
+    copy_c.start()
+    copy_c.wait()
     copy_h.wait()
-    copy_v.wait()
     halos(0)
 
     def build(r):
         @pl.loop(0, slots)
         def _(j):
             src, k = j // sc, j % sc
-            hr = hrecv[src, r, k, 0]
-            hi = hrecv[src, r, k, 1]
+            keep = jnp.where(idx[src, 0, r * sc + k] >= 0, 1.0, 0.0).astype(jnp.float32)
+            hr = (hrecv[src, r, k, 0].astype(jnp.float32) * keep).astype(jnp.bfloat16)
+            hi = (hrecv[src, r, k, 1].astype(jnp.float32) * keep).astype(jnp.bfloat16)
             first = pl.ds(pl.multiple_of(j * 2 * bs, bs), bs)
             second = pl.ds(pl.multiple_of(j * 2 * bs + bs, bs), bs)
             hc[r, 0:bs, first] = hr
@@ -145,18 +173,22 @@
 
     group = min(GROUP, slots)
 
+    def panel(r, j):
+        at = idx[j // sc, 0, r * sc + j % sc]
+        return jnp.where(at >= 0, at, rb)
+
     def product(n, r):
         def part(p):
             base = p * group
             rhs = jnp.concatenate(
-                [bufs[n - 1][idx[r * slots + base + u]] for u in range(group)], axis=0
+                [bufs[n - 1][panel(r, base + u)] for u in range(group)], axis=0
             )
             lhs = hc[r, :, pl.ds(pl.multiple_of(base * 2 * bs, 2 * bs), group * 2 * bs)]
             return jnp.dot(lhs, rhs, preferred_element_type=jnp.float32)
 
         if slots == group:
             return part(0)
-        zero = jnp.zeros((2 * bs, v0.shape[-1]), jnp.float32)
+        zero = jnp.zeros((2 * bs, width), jnp.float32)
         return lax.fori_loop(0, slots // group, lambda p, a: a + part(p), zero)
 
     for n in range(1, STEPS + 1):
@@ -166,6 +198,16 @@
                 @pl.loop(1, ns)
                 def _(d):
                     arrived(d, r).wait_recv()
+
+                @pl.when(r + ahead < R)
+                def _():
+                    @pl.loop(1, ns)
+                    def _(d):
+                        coupling(d, r).wait_send()
+
+                    @pl.loop(1, ns)
+                    def _(d):
+                        coupling(d, r + ahead).start()
 
                 build(r)
             t = product(n, r)
@@ -237,10 +279,9 @@
         total += mrow[i]
     mom_out[...] = total * scale
 
-    @pl.loop(0, R)
-    def _(r):
+    for r in range(R - ahead, R):
         @pl.loop(1, ns)
-        def _(d):
+        def _(d, r=r):
             coupling(d, r).wait_send()
 
     for n in range(STEPS + 1):
@@ -250,6 +291,12 @@
 
     pltpu.make_async_copy(ext3.at[pl.ds(rb, rb)], t3_out, local_sem.at[2]).wait()
     copy_t.wait()
+
+
+def widen(bs, t4, t3, last_vec, before_vec):
+    for src, dst in ((t4, last_vec), (t3, before_vec)):
+        for q in range(2):
+            dst[:, q, :] = src[0, q * bs : (q + 1) * bs, :].astype(jnp.float32)
 
 
 def body(nr, ns, start_vec, left_vec, hamil, cols, live):
@@ -258,22 +305,12 @@
     width = start_vec.shape[-1]
     R = rb // ns
     slots = sc * ns
-    s = lax.axis_index("section")
     base = lax.axis_index("rows") * rb
     scale = 1.0 / (2.0 * bs * rb) ** 0.5
 
-    def panels(x):
-        count = x.shape[0] // bs
-        return x.reshape(count, bs, 2, width).transpose(0, 2, 1, 3).reshape(count, 2 * bs, width)
-
-    def owned(x):
-        return panels(lax.dynamic_slice_in_dim(x, s * (R * bs), R * bs, axis=0))
-
-    v0 = panels(start_vec.astype(jnp.bfloat16))
     mask = jnp.arange(sc)[None, :] < live
-    hm = jnp.where(mask[:, :, None, None, None], hamil, jnp.zeros((), hamil.dtype))
-    every = lax.all_gather(cols, "section", axis=1, tiled=True)
-    idx = (lax.dynamic_slice_in_dim(every, s * R, R, axis=0) - base + rb).reshape(-1)
+    code = jnp.where(mask, cols - base + rb, -1).reshape(ns, 1, R * sc)
+    code = jnp.pad(code, ((0, 0), (0, 7), (0, -(R * sc) % 128)), constant_values=-1)
 
     dma = pltpu.SemaphoreType.DMA
     vmem = pl.BlockSpec(memory_space=pltpu.VMEM)
@@ -287,33 +324,42 @@
             jax.ShapeDtypeStruct((rb, 2 * bs, width), bf),
             jax.ShapeDtypeStruct((rb, 2 * bs, width), bf),
         ),
-        in_specs=[pl.BlockSpec(memory_space=pltpu.SMEM), anywhere, vmem, vmem, anywhere],
+        in_specs=[vmem, anywhere, anywhere, anywhere],
         out_specs=(vmem, anywhere, anywhere),
         scratch_shapes=[
+            pltpu.VMEM(start_vec.shape, f32),
+            pltpu.VMEM((R * bs, 2, width), f32),
+            pltpu.VMEM(code.shape, jnp.int32),
+            pltpu.SMEM(code.shape, jnp.int32),
             ext, ext, ext, ext,
             pltpu.VMEM((rb, 2 * bs, width), bf),
             pltpu.VMEM((ns, R, sc, 2, bs, bs), bf),
             pltpu.VMEM((R, 2 * bs, slots * 2 * bs), bf),
             pltpu.VMEM((2, R, 2 * bs, width), f32),
+            pltpu.VMEM((R, 2 * bs, width), f32),
             pltpu.VMEM((8, width), f32),
             pltpu.VMEM((ns, 8, width), f32),
             pltpu.VMEM((nr, 8, width), f32),
             dma((STEPS, rb)), dma((STEPS, rb)), dma((STEPS, rb)), dma((STEPS, rb)),
             dma((STEPS, rb)), dma((STEPS, rb)), dma((STEPS, rb)),
-            dma((ns, R)), dma((ns, R)),
-            dma((ns,)), dma((ns,)), dma((nr,)), dma((nr,)), dma((4,)),
+            dma((ns, R)), dma((ns, R)), dma((ns,)), dma((ns,)),
+            dma((ns,)), dma((ns,)), dma((nr,)), dma((nr,)), dma((6,)),
         ],
         compiler_params=pltpu.CompilerParams(
             collective_id=0, has_side_effects=True, vmem_limit_bytes=56 * 2**20
         ),
-    )(idx, v0, owned(start_vec), owned(left_vec), hm)
-
-    def whole(x):
-        return (
-            x.astype(f32).reshape(rb, 2, bs, width).transpose(0, 2, 1, 3).reshape(rb * bs, 2, width)
-        )
-
-    return mom[: STEPS + 1], whole(t4), whole(t3)
+    )(code, start_vec, left_vec, hamil)
+
+    taken = pl.BlockSpec((1, 2 * bs, width), lambda b: (b, 0, 0))
+    given = pl.BlockSpec((bs, 2, width), lambda b: (b, 0, 0))
+    last_vec, before_vec = pl.pallas_call(
+        functools.partial(widen, bs),
+        out_shape=(jax.ShapeDtypeStruct(start_vec.shape, f32),) * 2,
+        grid=(rb,),
+        in_specs=[taken, taken],
+        out_specs=(given, given),
+    )(t4, t3)
+    return mom[: STEPS + 1], last_vec, before_vec
 
 
 def solution(mesh):

time: 275 us -> 255 us (0.927)
  Pallas kernels: 234 us -> 252 us
  local copies, waits for them, and re-layouts: 18.7 us -> 1.38 us
  blocking collectives: 13.7 us -> 0 us
  other arithmetic: 7.26 us -> 0.69 us
    all_gather x1 -> x0, blocking collectives: 13.7 us -> none  [body(): every = lax.all_gather(cols, 'section', axis=1, tiled=True)]
    reshape x4 -> x1, local copies, waits for them, and re-layouts: 12.8 us -> 0.08 us  [body(): code = jnp.where(mask, cols - base + rb, -1).reshape(ns, 1, R * sc)]
    pallas_call x0 -> x1, Pallas kernels: none -> 11.5 us  [body(): pl.pallas_call(functools.partial(widen, bs), out_shape=(jax.ShapeDtypeStr...]
    pallas_call x1, Pallas kernels: 234 us -> 240 us  [body(): pl.pallas_call(functools.partial(kernel, nr, ns, slots, scale), out_shape...]
where the time goes in v2:
time: 255 us; the launch traced here: 254 us
  Pallas kernels  252 us (99%)
    pallas_call x1, Pallas kernels, body(): pl.pallas_call(functools.partial(kernel, nr, ns, slots, scale), out_shape...  240 us
    pallas_call x1, Pallas kernels, body(): pl.pallas_call(functools.partial(widen, bs), out_shape=(jax.ShapeDtypeStr...  11.5 us

profile of v2, /device:TPU:0, one launch (start us, length us, event | category | flops | bytes accessed | tf_op | source)
XLA Modules:
  0.0 254.4 jit_solution(4869731378353721475)
XLA Ops:
  0.6 0.7 add_select_fusion
  1.3 0.1 copy.10
  1.4 0.1 reshape.9
  1.5 0.6 pad.4.code
  2.1 240.1 %shard_map.76 = (f32[8,256]{1,0:T(8,128)}, bf16[16,256,256]{2,1,0:T(8,128)(2,1)}, bf16[16,256,256]{2,1,0:T(8,128)(2,1)}) custom-call(s32[4,8,128]{2,1,0:T(8,128)} %pad.4.code, f32[2048,2,256]{2,1,0:T(2,128)} %start_hbm.1, f32[2048,2,256]{2,1,0:T(2,128)} %left_hbm.1, bf16[16,4,2,128,128]{4,3,2,1,0:T(8,128)(2,1)} %hm.1), custom_call_target="tpu_custom_call" | custom-call | tf_op jit(solution)/shard_map/pallas_call | solution.py:320
  242.2 0.0 copy-start
  242.2 11.5 %shard_map.77 = (f32[2048,2,256]{2,1,0:T(2,128)}, f32[2048,2,256]{2,1,0:T(2,128)}) custom-call(bf16[16,256,256]{2,1,0:T(8,128)(2,1)} %get-tuple-element.9.t4, bf16[16,256,256]{2,1,0:T(8,128)(2,1)} %get-tuple-element.10.t3), custom_call_target="tpu_custom_call" | custom-call | tf_op jit(solution)/shard_map/pallas_call | solution.py:355
  253.8 0.0 copy-done
  253.8 0.6 copy.13
Async XLA Ops:
  242.2 11.5 %copy-start = (f32[8,256]{1,0:T(8,128)S(1)}, f32[8,256]{1,0:T(8,128)}, u32[]{:S(2)}) copy-start(f32[8,256]{1,0:T(8,128)} %get-tuple-element.8) | copy-start | bytes 24580

commit v3 on v2

--- a/solution.py
+++ b/solution.py
@@ -106,7 +106,7 @@
         to = lax.rem(s + d, ns)
         remote(code.at[to], codes.at[s], c_send.at[to], c_recv.at[s], (g, to)).start()
 
-    ahead = min(2, R)
+    ahead = min(4, R)
     for r in range(ahead):
         @pl.loop(1, ns)
         def _(d, r=r):
@@ -295,8 +295,10 @@
 
 def widen(bs, t4, t3, last_vec, before_vec):
     for src, dst in ((t4, last_vec), (t3, before_vec)):
-        for q in range(2):
-            dst[:, q, :] = src[0, q * bs : (q + 1) * bs, :].astype(jnp.float32)
+        for i in range(src.shape[0]):
+            for q in range(2):
+                part = src[i, q * bs : (q + 1) * bs, :]
+                dst[i * bs : (i + 1) * bs, q, :] = part.astype(jnp.float32)
 
 
 def body(nr, ns, start_vec, left_vec, hamil, cols, live):
@@ -350,12 +352,12 @@
         ),
     )(code, start_vec, left_vec, hamil)
 
-    taken = pl.BlockSpec((1, 2 * bs, width), lambda b: (b, 0, 0))
-    given = pl.BlockSpec((bs, 2, width), lambda b: (b, 0, 0))
+    taken = pl.BlockSpec((4, 2 * bs, width), lambda b: (b, 0, 0))
+    given = pl.BlockSpec((4 * bs, 2, width), lambda b: (b, 0, 0))
     last_vec, before_vec = pl.pallas_call(
         functools.partial(widen, bs),
         out_shape=(jax.ShapeDtypeStruct(start_vec.shape, f32),) * 2,
-        grid=(rb,),
+        grid=(rb // 4,),
         in_specs=[taken, taken],
         out_specs=(given, given),
     )(t4, t3)

time: 255 us -> 247 us (0.969)
  Pallas kernels: 252 us -> 244 us
    pallas_call x1, Pallas kernels: 11.5 us -> 6.71 us  [body(): pl.pallas_call(functools.partial(widen, bs), out_shape=(jax.ShapeDtypeStr...]
    pallas_call x1, Pallas kernels: 240 us -> 237 us  [body(): pl.pallas_call(functools.partial(kernel, nr, ns, slots, scale), out_shape...]
where the time goes in v3:
time: 247 us
  Pallas kernels  244 us (99%)
    pallas_call x1, Pallas kernels, body(): pl.pallas_call(functools.partial(kernel, nr, ns, slots, scale), out_shape...  237 us
    pallas_call x1, Pallas kernels, body(): pl.pallas_call(functools.partial(widen, bs), out_shape=(jax.ShapeDtypeStr...  6.71 us

profile of v3, /device:TPU:0, one launch (start us, length us, event | category | flops | bytes accessed | tf_op | source)
XLA Modules:
  0.0 246.8 jit_solution(17150991359135384280)
XLA Ops:
  0.6 0.7 add_select_fusion
  1.3 0.1 copy.10
  1.4 0.1 reshape.9
  1.5 0.6 pad.4.code
  2.1 237.4 %shard_map.76 = (f32[8,256]{1,0:T(8,128)}, bf16[16,256,256]{2,1,0:T(8,128)(2,1)}, bf16[16,256,256]{2,1,0:T(8,128)(2,1)}) custom-call(s32[4,8,128]{2,1,0:T(8,128)} %pad.4.code, f32[2048,2,256]{2,1,0:T(2,128)} %start_hbm.1, f32[2048,2,256]{2,1,0:T(2,128)} %left_hbm.1, bf16[16,4,2,128,128]{4,3,2,1,0:T(8,128)(2,1)} %hm.1), custom_call_target="tpu_custom_call" | custom-call | tf_op jit(solution)/shard_map/pallas_call | solution.py:322
  239.5 0.0 copy-start
  239.5 6.7 %shard_map.77 = (f32[2048,2,256]{2,1,0:T(2,128)}, f32[2048,2,256]{2,1,0:T(2,128)}) custom-call(bf16[16,256,256]{2,1,0:T(8,128)(2,1)} %get-tuple-element.9.t4, bf16[16,256,256]{2,1,0:T(8,128)(2,1)} %get-tuple-element.10.t3), custom_call_target="tpu_custom_call" | custom-call | tf_op jit(solution)/shard_map/pallas_call | solution.py:357
  246.2 0.0 copy-done
  246.2 0.6 copy.13
Async XLA Ops:
  239.5 6.7 %copy-start = (f32[8,256]{1,0:T(8,128)S(1)}, f32[8,256]{1,0:T(8,128)}, u32[]{:S(2)}) copy-start(f32[8,256]{1,0:T(8,128)} %get-tuple-element.8) | copy-start | bytes 24580

commit v4 on v3

--- a/solution.py
+++ b/solution.py
@@ -110,7 +110,7 @@
     for r in range(ahead):
         @pl.loop(1, ns)
         def _(d, r=r):
-            coupling(d, r).start()
+            coupling(ns - d, r).start()
 
     copy_v = pltpu.make_async_copy(start_hbm, stage, local_sem.at[1])
     copy_v.start()
@@ -191,6 +191,28 @@
         zero = jnp.zeros((2 * bs, width), jnp.float32)
         return lax.fori_loop(0, slots // group, lambda p, a: a + part(p), zero)
 
+    def gather(n, low, high):
+        @pl.loop(low, high)
+        def _(d):
+            @pl.loop(0, R)
+            def _(r):
+                @pl.when(s - d >= 0)
+                def _():
+                    c = (s - d) * R + r
+                    up(n, c).wait_recv()
+                    each(n, c, lambda x: x.start())
+
+                @pl.when(s + d < ns)
+                def _():
+                    c = (s + d) * R + r
+                    down(n, c).wait_recv()
+                    each(n, c, lambda x: x.start())
+
+                if n < STEPS:
+                    @pl.when(d == 1)
+                    def _():
+                        moment(n, r, tbuf[n % 2, r])
+
     for n in range(1, STEPS + 1):
         @pl.loop(0, R)
         def _(r, n=n):
@@ -220,7 +242,8 @@
             else:
                 bufs[n][rb + c] = t.astype(jnp.bfloat16)
             each(n, c, lambda x: x.start())
-            moment(n, r, t)
+            if n == STEPS:
+                moment(n, r, t)
 
         if n == STEPS:
             msec[s] = mloc[...]
@@ -230,29 +253,13 @@
                 to = lax.rem(s + d, ns)
                 remote(mloc, msec.at[s], m_send.at[to], m_recv.at[s], (g, to)).start()
 
-        @pl.loop(1, ns)
-        def _(d, n=n):
-            @pl.loop(0, R)
-            def _(r):
-                @pl.when(s - d >= 0)
-                def _():
-                    c = (s - d) * R + r
-                    up(n, c).wait_recv()
-                    each(n, c, lambda x: x.start())
-
-                @pl.when(s + d < ns)
-                def _():
-                    c = (s + d) * R + r
-                    down(n, c).wait_recv()
-                    each(n, c, lambda x: x.start())
-
         if n < STEPS:
+            gather(n, 1, ns)
             halos(n)
         if n == STEPS - 1:
             pltpu.make_async_copy(ext3.at[pl.ds(rb, rb)], t3_out, local_sem.at[2]).start()
 
-    copy_t = pltpu.make_async_copy(last, t4_out, local_sem.at[3])
-    copy_t.start()
+    gather(STEPS, 1, ns - 1)
 
     @pl.loop(1, ns)
     def _(d):
@@ -268,6 +275,10 @@
     def _(d):
         to = lax.rem(g + d, nr)
         remote(mrow.at[g], mrow.at[g], n_send.at[to], n_recv.at[g], (to, s)).start()
+
+    gather(STEPS, ns - 1, ns)
+    copy_t = pltpu.make_async_copy(last, t4_out, local_sem.at[3])
+    copy_t.start()
 
     @pl.loop(1, nr)
     def _(d):

time: 247 us -> 243 us (0.984)
  Pallas kernels: 244 us -> 240 us
    pallas_call x1, Pallas kernels: 237 us -> 233 us  [body(): pl.pallas_call(functools.partial(kernel, nr, ns, slots, scale), out_shape...]
where the time goes in v4:
time: 243 us
  Pallas kernels  240 us (99%)
    pallas_call x1, Pallas kernels, body(): pl.pallas_call(functools.partial(kernel, nr, ns, slots, scale), out_shape...  233 us
    pallas_call x1, Pallas kernels, body(): pl.pallas_call(functools.partial(widen, bs), out_shape=(jax.ShapeDtypeStr...  6.71 us

profile of v4, /device:TPU:0, one launch (start us, length us, event | category | flops | bytes accessed | tf_op | source)
XLA Modules:
  0.0 242.9 jit_solution(16133430775371714609)
XLA Ops:
  0.6 0.7 add_select_fusion
  1.3 0.1 copy.10
  1.4 0.1 reshape.9
  1.5 0.6 pad.4.code
  2.1 233.5 %shard_map.76 = (f32[8,256]{1,0:T(8,128)}, bf16[16,256,256]{2,1,0:T(8,128)(2,1)}, bf16[16,256,256]{2,1,0:T(8,128)(2,1)}) custom-call(s32[4,8,128]{2,1,0:T(8,128)} %pad.4.code, f32[2048,2,256]{2,1,0:T(2,128)} %start_hbm.1, f32[2048,2,256]{2,1,0:T(2,128)} %left_hbm.1, bf16[16,4,2,128,128]{4,3,2,1,0:T(8,128)(2,1)} %hm.1), custom_call_target="tpu_custom_call" | custom-call | tf_op jit(solution)/shard_map/pallas_call | solution.py:333
  235.6 0.0 copy-start
  235.6 6.7 %shard_map.77 = (f32[2048,2,256]{2,1,0:T(2,128)}, f32[2048,2,256]{2,1,0:T(2,128)}) custom-call(bf16[16,256,256]{2,1,0:T(8,128)(2,1)} %get-tuple-element.9.t4, bf16[16,256,256]{2,1,0:T(8,128)(2,1)} %get-tuple-element.10.t3), custom_call_target="tpu_custom_call" | custom-call | tf_op jit(solution)/shard_map/pallas_call | solution.py:368
  242.3 0.0 copy-done
  242.3 0.6 copy.13
Async XLA Ops:
  235.6 6.7 %copy-start = (f32[8,256]{1,0:T(8,128)S(1)}, f32[8,256]{1,0:T(8,128)}, u32[]{:S(2)}) copy-start(f32[8,256]{1,0:T(8,128)} %get-tuple-element.8) | copy-start | bytes 24580
